TPU v7x, 32 devices: a whole 2x2x4 slice. The times are simulated.
32 devices in a mesh: dp: 4 (over z), seq: 4 (over y, x), mp: 2 (over core).
Axes of the slice: x: 2, y: 2, z: 4, core: 2. Of those that a mesh axis runs over, the one named last changes fastest.
Arguments:
- queries: bfloat16 [4, 512, 768], P('dp', 'seq', 'mp'), may hold values from -60 to 60
- keys: bfloat16 [4, 512, 768], P('dp', 'seq', 'mp'), may hold values from -8 to 8
- values: bfloat16 [4, 512, 768], P('dp', 'seq', 'mp'), may hold values from -6 to 6
- proj_weight: bfloat16 [2, 384, 1536], P('mp', 'dp'), may hold values from -0.5 to 0.5
- gate_table: float32 [4, 1536], replicated, may hold values from -6 to 6
- timestep: int32 [4], P('dp'), may hold values from 0 to 3
- span_index: int32 [4], P('dp'), may hold values from 0 to 3
- cotangent: bfloat16 [4, 512, 1536], P('dp', 'seq'), may hold values from -0.0625 to 0.0625
Outputs:
- output: bfloat16 [4, 512, 1536], P('dp', ('seq', 'mp'))
- weight_grad: float32 [2, 4608, 128], P('mp', ('dp', 'seq'))
All inputs are finite; a program needn't handle non-finite values.
Results may differ from a plain program's by a relative error of at most 0.015.
Values may be sent and summed in bfloat16 or wider, within the bound.
A program may use at most 64 MiB of HBM per device.

v0:
```python
import jax
import jax.numpy as jnp
from jax import lax
from jax.sharding import PartitionSpec as P

HEAD = 128


def local(queries, keys, values, proj_weight, gate_table, timestep, span_index, cotangent):
    tok_rows = queries.shape[1]
    width = queries.shape[2]
    heads_here = width // HEAD
    inv_root = HEAD ** (-0.5)
    seq_place = lax.axis_index("seq")
    all_keys, all_values = (
        lax.all_gather(keys[0], "seq", axis=0, tiled=True),
        lax.all_gather(values[0], "seq", axis=0, tiled=True),
    )
    key_count = all_keys.shape[0]
    query_heads = queries[0].reshape(tok_rows, heads_here, HEAD)
    key_heads = all_keys.reshape(key_count, heads_here, HEAD)
    value_heads = all_values.reshape(key_count, heads_here, HEAD)
    scores = (
        jnp.einsum("qhd,khd->hqk", query_heads, key_heads, preferred_element_type=jnp.float32)
        * inv_root
    )
    key_span = jnp.arange(key_count, dtype=jnp.int32) // tok_rows
    visible = key_span <= jnp.minimum(seq_place, span_index[0])
    scores = jnp.where(visible[None, None, :], scores, -jnp.inf)
    row_top = jnp.max(scores, axis=2, keepdims=True)
    weights = jnp.exp(scores - row_top)
    probs = (weights / jnp.sum(weights, axis=2, keepdims=True)).astype(jnp.bfloat16)
    attended = jnp.einsum("hqk,khd->qhd", probs, value_heads, preferred_element_type=jnp.float32)
    attended = attended.reshape(tok_rows, width).astype(jnp.bfloat16)
    weight_rows = lax.all_gather(proj_weight, "dp", axis=1, tiled=True)
    mixed = jnp.dot(attended, weight_rows[0], preferred_element_type=jnp.float32)
    shared = lax.psum_scatter(
        mixed.astype(jnp.bfloat16), "mp", scatter_dimension=0, tiled=True
    ).astype(jnp.float32)
    step_hit = jnp.arange(gate_table.shape[0], dtype=jnp.int32) == timestep[0]
    gate = jnp.sum(jnp.where(step_hit[:, None], gate_table, 0.0), axis=0)
    output = (gate[None, :] * shared).astype(jnp.bfloat16)[None]
    scaled = (gate[None, :] * cotangent[0].astype(jnp.float32)).astype(jnp.bfloat16)
    term = jnp.dot(attended.T, scaled, preferred_element_type=jnp.float32).reshape(-1, 128)
    rows_all = term.shape[0]
    dp_count = lax.axis_size("dp")
    seq_count = lax.axis_size("seq")
    block_rows = rows_all // (dp_count * seq_count)
    grid_view = term.reshape(dp_count, seq_count, block_rows, 128)
    local_sum = lax.psum_scatter(
        grid_view.transpose(1, 0, 2, 3)
        .reshape(lax.axis_size("seq") * (rows_all // seq_count), 128)
        .astype(jnp.bfloat16),
        "seq",
        scatter_dimension=0,
        tiled=True,
    ).astype(jnp.float32)
    piece = lax.psum_scatter(local_sum, "dp", scatter_dimension=0, tiled=True)
    return (output, piece[None])


def solution(mesh):
    return jax.shard_map(
        local,
        mesh=mesh,
        in_specs=(
            P("dp", "seq", "mp"),
            P("dp", "seq", "mp"),
            P("dp", "seq", "mp"),
            P("mp", "dp", None),
            P(),
            P("dp"),
            P("dp"),
            P("dp", "seq", None),
        ),
        out_specs=(P("dp", ("seq", "mp"), None), P("mp", ("dp", "seq"), None)),
        check_vma=False,
    )
```

profile of v0, /device:TPU:0, one launch (start us, length us, event | category | flops | bytes accessed | tf_op | source)
XLA Modules:
  0.0 110.6 jit_solution(10646305211684677769)
XLA Ops:
  8.0 0.0 copy-start.1
  8.0 0.0 all-gather.4.cloned.1.call-start
  8.1 0.7 all-gather.4.cloned.1.call-update
  8.7 0.0 reduce-scatter.6.cloned.1.call-start
  8.8 1.0 copy.14
  9.8 1.0 copy.13
  11.5 11.3 %all-gather.1 = bf16[1,512,384]{2,1,0:T(8,128)(2,1)S(1)} all-gather(bf16[1,128,384]{2,1,0:T(8,128)(2,1)} %param.10), channel_id=3, replica_groups=mesh['dp'=4,'seq'=4,'mp'=2] {'seq'}, dimensions={1}, use_global_device_ids=true | all-gather | bytes 491520 | tf_op jit(solution)/shard_map/all_gather | solution.py:17
  22.8 0.2 copy.17
  23.6 9.7 %all-gather = bf16[1,512,384]{1,2,0:T(8,128)(2,1)S(1)} all-gather(bf16[1,128,384]{1,2,0:T(8,128)(2,1)S(1)} %copy.14), channel_id=2, replica_groups=mesh['dp'=4,'seq'=4,'mp'=2] {'seq'}, dimensions={1}, use_global_device_ids=true | all-gather | bytes 491520 | tf_op jit(solution)/shard_map/all_gather | solution.py:16
  33.3 0.0 copy-done.1
  33.4 0.1 select_reduce_fusion
  33.5 0.5 fusion.16
  33.9 0.3 fusion.3
  34.3 0.0 copy-start
  34.3 0.9 convolution_convert_fusion.2
  35.1 0.1 copy-done
  35.3 0.5 convolution_convert_fusion
  35.7 1.4 %convert_element_type.58 = bf16[4,4,288,128]{3,2,1,0:T(8,128)(2,1)S(1)} reshape(bf16[384,1536]{1,0:T(8,128)(2,1)S(1)} %convolution_convert_fusion) | data formatting | bytes 2359296 | tf_op jit(solution)/shard_map/convert_element_type | solution.py:53
  37.2 1.1 copy.18
  38.2 0.0 reduce-scatter.6.cloned.1.call-update
  38.3 0.0 reduce-scatter.4.cloned.1.call-start
  38.3 5.3 %all-gather.4.cloned.1.call-done = bf16[1,384,1536]{2,1,0:T(8,128)(2,1)} async-done(((bf16[1,96,1536]{2,1,0:T(8,128)(2,1)}), bf16[1,384,1536]{2,1,0:T(8,128)(2,1)}) %all-gather.4.cloned.1.call-update) | async-done | bytes 1179664 | tf_op jit(solution)/shard_map/all_gather | solution.py:35
  43.6 2.4 %convolution_convert_fusion.1 = bf16[128,1536]{1,0:T(8,128)(2,1)} fusion(bf16[128,384]{0,1:T(8,128)(2,1)S(1)} %bitcast.34, bf16[1,384,1536]{2,1,0:T(8,128)(2,1)} %all-gather.4.cloned.1.call-done), kind=kOutput, calls=%fused_computation.2 | convolution fusion | flops 151191552 | bytes 1671168 | tf_op jit(solution)/shard_map/dot_general | solution.py:36
  46.0 0.0 reduce-scatter.4.cloned.1.call-update
  46.0 0.0 reduce-scatter.8.cloned.1.call-start
  46.1 21.1 %reduce-scatter.6.cloned.1.call-done = bf16[1152,128]{1,0:T(8,128)(2,1)} async-done(((bf16[4608,128]{1,0:T(8,128)(2,1)}), bf16[1152,128]{1,0:T(8,128)(2,1)}) %reduce-scatter.6.cloned.1.call-update) | async-done | bytes 294928 | tf_op jit(solution)/shard_map/reduce_scatter | solution.py:50
  67.2 1.8 %convert_element_type.61 = f32[1152,128]{1,0:T(8,128)} convert(bf16[1152,128]{1,0:T(8,128)(2,1)} %reduce-scatter.6.cloned.1.call-done) | non-fusion elementwise | flops 147456 | bytes 884736 | tf_op jit(solution)/shard_map/convert_element_type | solution.py:57
  69.0 0.0 reduce-scatter.8.cloned.1.call-update
  69.0 8.0 %reduce-scatter.4.cloned.1.call-done = bf16[64,1536]{1,0:T(8,128)(2,1)} async-done(((bf16[128,1536]{1,0:T(8,128)(2,1)}), bf16[64,1536]{1,0:T(8,128)(2,1)}) %reduce-scatter.4.cloned.1.call-update) | async-done | bytes 196624 | tf_op jit(solution)/shard_map/reduce_scatter | solution.py:37
  77.0 1.6 %fusion.8 = bf16[1,64,1536]{2,1,0:T(8,128)(2,1)} fusion(bf16[64,1536]{1,0:T(8,128)(2,1)} %reduce-scatter.4.cloned.1.call-done, f32[1536]{0:T(1024)S(1)} %select_reduce_fusion), kind=kLoop, calls=%fused_computation.14 | loop fusion | flops 294912 | bytes 399360 | tf_op jit(solution)/shard_map/broadcast_in_dim | solution.py:42
  78.7 24.3 %reduce-scatter.8.cloned.1.call-done = f32[288,128]{1,0:T(8,128)} async-done(((f32[1152,128]{1,0:T(8,128)}), f32[288,128]{1,0:T(8,128)}) %reduce-scatter.8.cloned.1.call-update) | async-done | bytes 147472 | tf_op jit(solution)/shard_map/reduce_scatter | solution.py:58
  (2 shorter events, 0.0 us)
Async XLA Ops:
  8.0 25.4 %copy-start.1 = (f32[4,1536]{1,0:T(4,128)S(1)}, f32[4,1536]{1,0:T(4,128)}, u32[]{:S(2)}) copy-start(f32[4,1536]{1,0:T(4,128)} %param.12) | copy-start | bytes 73732
  8.0 35.6 %all-gather.4.cloned.1.call-start = ((), (), s32[]{:S(2)}) async-start(), calls=%async_computation.3 | async-start | bytes 1474560 | tf_op jit(solution)/shard_map/all_gather | solution.py:35
  8.7 58.4 %reduce-scatter.6.cloned.1.call-start = ((), (), s32[]{:S(2)}) async-start(), calls=%async_computation.5 | async-start | bytes 1474560 | tf_op jit(solution)/shard_map/reduce_scatter | solution.py:50
  34.3 1.0 copy-start
  38.3 38.8 %reduce-scatter.4.cloned.1.call-start = ((), (), s32[]{:S(2)}) async-start(), calls=%async_computation.4 | async-start | bytes 589824 | tf_op jit(solution)/shard_map/reduce_scatter | solution.py:37
  46.0 57.0 %reduce-scatter.8.cloned.1.call-start = ((), (), s32[]{:S(2)}) async-start(), calls=%async_computation.6 | async-start | bytes 737280 | tf_op jit(solution)/shard_map/reduce_scatter | solution.py:58
Sparse Core Ops, SparseCore 0:
  10.4 33.1 all-gather.3
Sparse Core Ops, SparseCore 1:
  38.3 28.8 reduce-scatter.5
  69.3 7.7 reduce-scatter.3
  79.9 23.1 reduce-scatter.7
where the time goes:
time: 111 us
  waiting for transfers between devices  59.4 us (54%)
  blocking collectives  21 us (19%)
  between operations  17.1 us (15%)
  local copies, waits for them, and re-layouts  4.83 us (4%)
  matrix products  4.54 us (4%)
  other arithmetic  3.55 us (3%)
    reduce_scatter x1, waiting for transfers between devices, local(): piece = lax.psum_scatter(local_sum, 'dp', scatter_dimension=0, tiled=True)  24.3 us
    reduce_scatter x1, waiting for transfers between devices, local(): lax.psum_scatter(grid_view.transpose(1, 0, 2, 3).reshape(lax.axis_size('s...  21.1 us
    all_gather x1, blocking collectives, local(): lax.all_gather(values[0], 'seq', axis=0, tiled=True)  11.3 us
    all_gather x1, blocking collectives, local(): lax.all_gather(keys[0], 'seq', axis=0, tiled=True)  9.69 us
    reduce_scatter x1, waiting for transfers between devices, local(): lax.psum_scatter(mixed.astype(jnp.bfloat16), 'mp', scatter_dimension=0, t...  8 us
    all_gather x1, waiting for transfers between devices, local(): weight_rows = lax.all_gather(proj_weight, 'dp', axis=1, tiled=True)  5.27 us
    convert_element_type x2, local copies, waits for them, and re-layouts, local(): local_sum = lax.psum_scatter(grid_view.transpose(1, 0, 2, 3).reshape(lax....  2.5 us
    dot_general x1, matrix products, local(): jnp.dot(attended, weight_rows[0], preferred_element_type=jnp.float32)  2.41 us
  transfers between devices with their start and end apart: 4, of which 4 were waited for; matrix products, arithmetic and copies ran while one was open for 12% of the time, Pallas kernels for 0%

commit v1 on v0

--- a/solution.py
+++ b/solution.py
@@ -1,9 +1,249 @@
+import functools
+
 import jax
 import jax.numpy as jnp
 from jax import lax
+from jax.experimental import pallas as pl
+from jax.experimental.pallas import tpu as pltpu
 from jax.sharding import PartitionSpec as P
 
 HEAD = 128
+MESH = pl.DeviceIdType.MESH
+PLANE = 4
+CHUNKS = 2
+
+
+def fused(dp_count, q_ref, k_ref, v_ref, w_ref, gate_ref, time_ref, span_ref, cot_ref,
+          out_ref, grad_ref,
+          kbuf, vbuf, wbuf, cbuf, attn, asend, abuf, gbuf, rsend, rbuf, mix, msend, mrecv, grow,
+          local_sem, send_sem, recv_sem):
+    tok, width = q_ref.shape
+    model = cot_ref.shape[1]
+    wrows = w_ref.shape[0]
+    wcols = model // PLANE
+    half = tok // 2
+    piece = width // (dp_count * PLANE)
+    part = model // CHUNKS
+    heads = width // HEAD
+    d, s, m = lax.axis_index("dp"), lax.axis_index("seq"), lax.axis_index("mp")
+    x, y = lax.rem(s, 2), s // 2
+
+    def at(mx, my):
+        return lax.rem(y + my, 2) * 2 + lax.rem(x + mx, 2)
+
+    first, second, far = at(1 - m, m), at(m, 1 - m), at(1, 1)
+    dev = {p: (d, i, m) for p, i in (("a", first), ("b", second), ("c", far))}
+    sibling = (d, s, 1 - m)
+    depth = [lax.rem(d + o, dp_count) for o in range(dp_count)]
+    depth_from = [lax.rem(d + dp_count - o, dp_count) for o in range(dp_count)]
+
+    names = {}
+    sent = []
+
+    def remote(name, src, dst, target):
+        i = names.setdefault(name, len(names))
+        return pltpu.make_async_remote_copy(
+            src_ref=src, dst_ref=dst, send_sem=send_sem.at[i], recv_sem=recv_sem.at[i],
+            device_id=target, device_id_type=MESH)
+
+    def send(name, src, dst, target):
+        copy = remote(name, src, dst, target)
+        copy.start()
+        sent.append(copy)
+
+    def arrive(name, dst):
+        remote(name, dst, dst, sibling).wait_recv()
+
+    def wrow(i):
+        return pl.ds(pl.multiple_of(i * wrows, 16), wrows)
+
+    def wcol(i):
+        return pl.ds(pl.multiple_of(i * wcols, 128), wcols)
+
+    mine = pl.ds(pl.multiple_of(m * half, 16), half)
+    other = pl.ds(pl.multiple_of((1 - m) * half, 16), half)
+
+    local = [
+        pltpu.make_async_copy(k_ref, kbuf.at[s], local_sem.at[0]),
+        pltpu.make_async_copy(v_ref, vbuf.at[s], local_sem.at[1]),
+        pltpu.make_async_copy(cot_ref, cbuf.at[s], local_sem.at[2]),
+    ] + [
+        pltpu.make_async_copy(
+            w_ref.at[:, i * wcols:(i + 1) * wcols], wbuf.at[i, wrow(d)], local_sem.at[3 + i])
+        for i in range(PLANE)
+    ]
+
+    barrier = pltpu.get_barrier_semaphore()
+    partners = [dev["a"], dev["b"], dev["c"], sibling] + [
+        (depth[o], s, m) for o in range(1, dp_count)]
+    for target in partners:
+        pl.semaphore_signal(barrier, inc=1, device_id=target, device_id_type=MESH)
+    for copy in local:
+        copy.start()
+    table = gate_ref[...]
+    hit = lax.broadcasted_iota(jnp.int32, table.shape, 0) == time_ref[0]
+    grow[...] = jnp.sum(jnp.where(hit, table, 0.0), axis=0, keepdims=True)
+    pl.semaphore_wait(barrier, len(partners))
+
+    for p in ("a", "b"):
+        send("k" + p, k_ref, kbuf.at[s], dev[p])
+        send("v" + p, v_ref, vbuf.at[s], dev[p])
+    for o in range(1, dp_count):
+        send(f"wz{o}", w_ref.at[:, wcol(s)], wbuf.at[s, wrow(d)], (depth[o], s, m))
+
+    arrive("ka", kbuf.at[first])
+    send("kc", kbuf.at[first], kbuf.at[first], dev["b"])
+    arrive("va", vbuf.at[first])
+    send("vc", vbuf.at[first], vbuf.at[first], dev["b"])
+    for p in ("a", "b"):
+        send("t" + p, cot_ref.at[mine], cbuf.at[s, mine], dev[p])
+    local[0].wait()
+    local[1].wait()
+    arrive("kb", kbuf.at[second])
+    arrive("vb", vbuf.at[second])
+    arrive("kc", kbuf.at[far])
+    arrive("vc", vbuf.at[far])
+
+    limit = jnp.minimum(s, span_ref[0])
+    visible = lax.broadcasted_iota(jnp.int32, (PLANE, tok, tok), 0) <= limit
+    columns = []
+    for h in range(heads):
+        lanes = slice(h * HEAD, (h + 1) * HEAD)
+        keys = kbuf[:, :, lanes].reshape(PLANE * tok, HEAD)
+        values = vbuf[:, :, lanes].reshape(PLANE * tok, HEAD)
+        scores = lax.dot_general(
+            keys, q_ref[:, lanes], (((1,), (1,)), ((), ())),
+            preferred_element_type=jnp.float32) * (HEAD ** -0.5)
+        scores = jnp.where(visible, scores.reshape(PLANE, tok, tok), -jnp.inf)
+        scores = scores.reshape(PLANE * tok, tok)
+        weights = jnp.exp(scores - jnp.max(scores, axis=0, keepdims=True))
+        total = jnp.sum(weights, axis=0, keepdims=True)
+        probs = (weights / total).astype(jnp.bfloat16)
+        columns.append(lax.dot_general(
+            values, probs, (((0,), (0,)), ((), ())), preferred_element_type=jnp.float32))
+    turned = jnp.concatenate(columns, axis=0)
+    attn[...] = turned.astype(jnp.bfloat16)
+    grouped = turned.reshape(dp_count, PLANE, piece, tok)
+    for t in range(PLANE):
+        asend[t] = grouped[:, t].reshape(dp_count * piece, tok).astype(jnp.bfloat16)
+    for p, i in (("c", far), ("a", first), ("b", second)):
+        send("o" + p, asend.at[i], abuf.at[s], dev[p])
+    abuf[s] = asend[s]
+
+    arrive("ta", cbuf.at[first, mine])
+    send("tc", cbuf.at[first, mine], cbuf.at[first, mine], dev["b"])
+    send("sa", cbuf.at[first, mine], cbuf.at[first, mine], sibling)
+    for o in range(1, dp_count):
+        block = wbuf.at[s, wrow(depth_from[o])]
+        arrive(f"wz{o}", block)
+        for p in ("a", "b"):
+            send(f"w{p}{o}", block, block, dev[p])
+    arrive("tb", cbuf.at[second, mine])
+    send("sb", cbuf.at[second, mine], cbuf.at[second, mine], sibling)
+
+    def project(slot, column):
+        mix[slot] = lax.dot_general(
+            attn[...], wbuf[column], (((0,), (0,)), ((), ())),
+            preferred_element_type=jnp.float32)
+        msend[slot] = mix[slot, other].astype(jnp.bfloat16)
+        send(f"m{slot}", msend.at[slot], mrecv.at[slot], sibling)
+
+    for copy in local[2:]:
+        copy.wait()
+    project(0, s)
+
+    arrive("tc", cbuf.at[far, mine])
+    send("sc", cbuf.at[far, mine], cbuf.at[far, mine], sibling)
+    for p, i in (("c", far), ("a", first), ("b", second)):
+        arrive("o" + p, abuf.at[i])
+    for p, i in (("a", second), ("b", first), ("c", far)):
+        arrive("s" + p, cbuf.at[i, other])
+
+    rows = jnp.concatenate([abuf[j] for j in range(PLANE)], axis=1)
+    for c in range(CHUNKS):
+        lanes = slice(c * part, (c + 1) * part)
+        term = jnp.dot(
+            rows, cbuf[:, :, lanes].reshape(PLANE * tok, part),
+            preferred_element_type=jnp.float32) * grow[:, lanes]
+        term = term.reshape(dp_count, piece, part)
+        gbuf[:, :, lanes] = term
+        stacked = jnp.concatenate(
+            [term[:, :, :part // 2], term[:, :, part // 2:]], axis=1).astype(jnp.bfloat16)
+        rsend[c] = stacked
+        for o in range(1, dp_count):
+            send(f"r{c}{o}", rsend.at[c, depth[o]], rbuf.at[c, o - 1], (depth[o], s, m))
+
+    for o in range(1, dp_count):
+        block = wbuf.at[first, wrow(depth_from[o])]
+        arrive(f"wa{o}", block)
+        send(f"wc{o}", block, block, dev["b"])
+    for o in range(1, dp_count):
+        arrive(f"wb{o}", wbuf.at[second, wrow(depth_from[o])])
+    project(1, at(1, 0))
+    project(2, at(0, 1))
+    for o in range(1, dp_count):
+        arrive(f"wc{o}", wbuf.at[far, wrow(depth_from[o])])
+    project(3, far)
+
+    for c in range(CHUNKS):
+        lanes = slice(c * part, (c + 1) * part)
+        total = gbuf[d, :, lanes]
+        for o in range(1, dp_count):
+            arrive(f"r{c}{o}", rbuf.at[c, o - 1])
+            got = rbuf[c, o - 1].astype(jnp.float32)
+            total += jnp.concatenate([got[:piece], got[piece:]], axis=1)
+        grad_ref[:, lanes] = total
+
+    for slot, column in enumerate((s, at(1, 0), at(0, 1), far)):
+        arrive(f"m{slot}", mrecv.at[slot])
+        whole = mix[slot, mine] + mrecv[slot].astype(jnp.float32)
+        out_ref[:, wcol(column)] = (grow[:, wcol(column)] * whole).astype(jnp.bfloat16)
+    for copy in sent:
+        copy.wait_send()
+
+
+def fused_local(dp_count, queries, keys, values, proj_weight, gate_table, timestep, span_index, cotangent):
+    tok, width = queries.shape[1:]
+    model = cotangent.shape[2]
+    wrows = proj_weight.shape[1]
+    piece = width // (dp_count * PLANE)
+    bf16, f32 = jnp.bfloat16, jnp.float32
+    vmem = pl.BlockSpec(memory_space=pltpu.VMEM)
+    smem = pl.BlockSpec(memory_space=pltpu.SMEM)
+    anywhere = pl.BlockSpec(memory_space=pl.ANY)
+    part = model // CHUNKS
+    copies = 16 + 4 + (dp_count - 1) * (4 + CHUNKS)
+    output, grad = pl.pallas_call(
+        functools.partial(fused, dp_count),
+        out_shape=(
+            jax.ShapeDtypeStruct((tok // 2, model), bf16),
+            jax.ShapeDtypeStruct((piece, model), f32),
+        ),
+        in_specs=[vmem, anywhere, anywhere, anywhere, vmem, smem, smem, anywhere],
+        out_specs=(vmem, vmem),
+        scratch_shapes=[
+            pltpu.VMEM((PLANE, tok, width), bf16),
+            pltpu.VMEM((PLANE, tok, width), bf16),
+            pltpu.VMEM((PLANE, dp_count * wrows, model // PLANE), bf16),
+            pltpu.VMEM((PLANE, tok, model), bf16),
+            pltpu.VMEM((width, tok), bf16),
+            pltpu.VMEM((PLANE, dp_count * piece, tok), bf16),
+            pltpu.VMEM((PLANE, dp_count * piece, tok), bf16),
+            pltpu.VMEM((dp_count, piece, model), f32),
+            pltpu.VMEM((CHUNKS, dp_count, 2 * piece, part // 2), bf16),
+            pltpu.VMEM((CHUNKS, dp_count - 1, 2 * piece, part // 2), bf16),
+            pltpu.VMEM((PLANE, tok, model // PLANE), f32),
+            pltpu.VMEM((PLANE, tok // 2, model // PLANE), bf16),
+            pltpu.VMEM((PLANE, tok // 2, model // PLANE), bf16),
+            pltpu.VMEM((1, model), f32),
+            pltpu.SemaphoreType.DMA((3 + PLANE,)),
+            pltpu.SemaphoreType.DMA((copies,)),
+            pltpu.SemaphoreType.DMA((copies,)),
+        ],
+        compiler_params=pltpu.CompilerParams(
+            collective_id=0, has_side_effects=True, vmem_limit_bytes=48 * 2**20),
+    )(queries[0], keys[0], values[0], proj_weight[0], gate_table, timestep, span_index, cotangent[0])
+    return output[None], grad.reshape(1, -1, 128)
 
 
 def local(queries, keys, values, proj_weight, gate_table, timestep, span_index, cotangent):
@@ -60,8 +300,9 @@
 
 
 def solution(mesh):
+    small = mesh.shape["seq"] == PLANE and mesh.shape["mp"] == 2 and mesh.shape["dp"] == 4
     return jax.shard_map(
-        local,
+        functools.partial(fused_local, mesh.shape["dp"]) if small else local,
         mesh=mesh,
         in_specs=(
             P("dp", "seq", "mp"),

time: 111 us -> 41.8 us (0.38)
  the two profiles are of different devices: /device:TPU:0 before, /device:TPU:1 now
where the time goes in v1:
time: 41.8 us; the launch traced here: 41.5 us
  Pallas kernels  32.8 us (78%)
  local copies, waits for them, and re-layouts  6.71 us (16%)
  between operations  1.95 us (5%)
    pallas_call x1, Pallas kernels, fused_local(): pl.pallas_call(functools.partial(fused, dp_count), out_shape=(jax.ShapeDt...  32.8 us
    unnamed x13, local copies, waits for them, and re-layouts  6.04 us

profile of v1, /device:TPU:1, one launch (start us, length us, event | category | flops | bytes accessed | tf_op | source)
XLA Modules:
  0.0 41.5 jit_solution(7603301534137335944)
XLA Ops:
  1.9 0.0 copy-start
  1.9 1.0 %copy-done = bf16[1,128,1536]{2,1,0:T(8,128)(2,1)S(1)} copy-done((bf16[1,128,1536]{2,1,0:T(8,128)(2,1)S(1)}, bf16[1,128,1536]{2,1,0:T(8,128)(2,1)}, u32[]{:S(2)}) %copy-start) | copy-done | bytes 393240
  2.9 0.0 copy-start.1
  2.9 1.0 %copy-done.1 = bf16[1,96,1536]{2,1,0:T(8,128)(2,1)S(1)} copy-done((bf16[1,96,1536]{2,1,0:T(8,128)(2,1)S(1)}, bf16[1,96,1536]{2,1,0:T(8,128)(2,1)}, u32[]{:S(2)}) %copy-start.1) | copy-done | bytes 294936
  3.9 0.0 copy-start.2
  3.9 0.9 %copy-done.2 = bf16[1,128,384]{2,1,0:T(8,128)(2,1)S(1)} copy-done((bf16[1,128,384]{2,1,0:T(8,128)(2,1)S(1)}, bf16[1,128,384]{2,1,0:T(8,128)(2,1)}, u32[]{:S(2)}) %copy-start.2) | copy-done | bytes 98328
  4.8 0.0 copy-start.3
  4.8 0.9 %copy-done.3 = bf16[1,128,384]{2,1,0:T(8,128)(2,1)S(1)} copy-done((bf16[1,128,384]{2,1,0:T(8,128)(2,1)S(1)}, bf16[1,128,384]{2,1,0:T(8,128)(2,1)}, u32[]{:S(2)}) %copy-start.3) | copy-done | bytes 98328
  5.7 0.0 copy-start.4
  5.7 0.9 %copy-done.4 = bf16[1,128,384]{2,1,0:T(8,128)(2,1)S(1)} copy-done((bf16[1,128,384]{2,1,0:T(8,128)(2,1)S(1)}, bf16[1,128,384]{2,1,0:T(8,128)(2,1)}, u32[]{:S(2)}) %copy-start.4) | copy-done | bytes 98328
  6.6 0.0 copy-start.5
  6.6 0.7 %copy-done.5 = f32[4,1536]{1,0:T(4,128)S(1)} copy-done((f32[4,1536]{1,0:T(4,128)S(1)}, f32[4,1536]{1,0:T(4,128)}, u32[]{:S(2)}) %copy-start.5) | copy-done | bytes 24600
  7.3 32.8 %shard_map.95 = (bf16[64,1536]{1,0:T(8,128)(2,1)S(1)}, f32[24,1536]{1,0:T(8,128)S(1)}) custom-call(bf16[128,384]{1,0:T(8,128)(2,1)S(1)} %bitcast.9, bf16[128,384]{1,0:T(8,128)(2,1)S(1)} %bitcast.10, bf16[128,384]{1,0:T(8,128)(2,1)S(1)} %bitcast.11, bf16[96,1536]{1,0:T(8,128)(2,1)S(1)} %bitcast.7, f32[4,1536]{1,0:T(4,128)S(1)} %copy-done.5, ...), custom_call_target="tpu_custom_call" | custom-call | tf_op jit(solution)/shard_map/pallas_call | solution.py:216
  40.1 0.7 %reshape.7 = f32[1,288,128]{2,1,0:T(8,128)} reshape(f32[24,1536]{1,0:T(8,128)S(1)} %get-tuple-element.5) | data formatting | bytes 294912 | tf_op jit(solution)/shard_map/reshape | solution.py:246
  40.8 0.7 %copy.13 = bf16[1,64,1536]{2,1,0:T(8,128)(2,1)} copy(bf16[1,64,1536]{2,1,0:T(8,128)(2,1)S(1)} %bitcast.8) | data formatting | bytes 393216
Async XLA Ops:
  1.9 1.0 %copy-start = (bf16[1,128,1536]{2,1,0:T(8,128)(2,1)S(1)}, bf16[1,128,1536]{2,1,0:T(8,128)(2,1)}, u32[]{:S(2)}) copy-start(bf16[1,128,1536]{2,1,0:T(8,128)(2,1)} %param.15) | copy-start | bytes 1179652
  2.9 1.0 %copy-start.1 = (bf16[1,96,1536]{2,1,0:T(8,128)(2,1)S(1)}, bf16[1,96,1536]{2,1,0:T(8,128)(2,1)}, u32[]{:S(2)}) copy-start(bf16[1,96,1536]{2,1,0:T(8,128)(2,1)} %param.11) | copy-start | bytes 884740
  3.9 0.9 %copy-start.2 = (bf16[1,128,384]{2,1,0:T(8,128)(2,1)S(1)}, bf16[1,128,384]{2,1,0:T(8,128)(2,1)}, u32[]{:S(2)}) copy-start(bf16[1,128,384]{2,1,0:T(8,128)(2,1)} %param.8) | copy-start | bytes 294916
  4.8 0.9 %copy-start.3 = (bf16[1,128,384]{2,1,0:T(8,128)(2,1)S(1)}, bf16[1,128,384]{2,1,0:T(8,128)(2,1)}, u32[]{:S(2)}) copy-start(bf16[1,128,384]{2,1,0:T(8,128)(2,1)} %param.9) | copy-start | bytes 294916
  5.7 0.9 %copy-start.4 = (bf16[1,128,384]{2,1,0:T(8,128)(2,1)S(1)}, bf16[1,128,384]{2,1,0:T(8,128)(2,1)}, u32[]{:S(2)}) copy-start(bf16[1,128,384]{2,1,0:T(8,128)(2,1)} %param.10) | copy-start | bytes 294916
  6.6 0.7 %copy-start.5 = (f32[4,1536]{1,0:T(4,128)S(1)}, f32[4,1536]{1,0:T(4,128)}, u32[]{:S(2)}) copy-start(f32[4,1536]{1,0:T(4,128)} %gate_ref.1) | copy-start | bytes 73732

commit v2 on v1

--- a/solution.py
+++ b/solution.py
@@ -13,11 +13,11 @@
 CHUNKS = 2
 
 
-def fused(dp_count, q_ref, k_ref, v_ref, w_ref, gate_ref, time_ref, span_ref, cot_ref,
+def fused(dp_count, q_hbm, k_ref, v_ref, w_ref, gate_hbm, time_ref, span_ref, cot_ref,
           out_ref, grad_ref,
-          kbuf, vbuf, wbuf, cbuf, attn, asend, abuf, gbuf, rsend, rbuf, mix, msend, mrecv, grow,
+          q_ref, gate_ref, kbuf, vbuf, wbuf, cbuf, attn, sbuf, tbuf, asend, abuf, gbuf, rsend, rbuf, mix, msend, mrecv, grow,
           local_sem, send_sem, recv_sem):
-    tok, width = q_ref.shape
+    tok, width = q_hbm.shape
     model = cot_ref.shape[1]
     wrows = w_ref.shape[0]
     wcols = model // PLANE
@@ -72,63 +72,86 @@
             w_ref.at[:, i * wcols:(i + 1) * wcols], wbuf.at[i, wrow(d)], local_sem.at[3 + i])
         for i in range(PLANE)
     ]
+    early = [
+        pltpu.make_async_copy(gate_hbm, gate_ref, local_sem.at[3 + PLANE]),
+        pltpu.make_async_copy(q_hbm, q_ref, local_sem.at[4 + PLANE]),
+    ]
 
     barrier = pltpu.get_barrier_semaphore()
     partners = [dev["a"], dev["b"], dev["c"], sibling] + [
         (depth[o], s, m) for o in range(1, dp_count)]
     for target in partners:
         pl.semaphore_signal(barrier, inc=1, device_id=target, device_id_type=MESH)
-    for copy in local:
+    for copy in early + local:
         copy.start()
+    pl.semaphore_wait(barrier, len(partners))
+
+    for p in ("a", "b"):
+        send("k" + p, k_ref, kbuf.at[s], dev[p])
+    for p in ("a", "b"):
+        send("v" + p, v_ref, vbuf.at[s], dev[p])
+    for o in range(1, dp_count):
+        send(f"wz{o}", w_ref.at[:, wcol(s)], wbuf.at[s, wrow(d)], (depth[o], s, m))
+
+    early[0].wait()
     table = gate_ref[...]
     hit = lax.broadcasted_iota(jnp.int32, table.shape, 0) == time_ref[0]
     grow[...] = jnp.sum(jnp.where(hit, table, 0.0), axis=0, keepdims=True)
-    pl.semaphore_wait(barrier, len(partners))
-
-    for p in ("a", "b"):
-        send("k" + p, k_ref, kbuf.at[s], dev[p])
-        send("v" + p, v_ref, vbuf.at[s], dev[p])
-    for o in range(1, dp_count):
-        send(f"wz{o}", w_ref.at[:, wcol(s)], wbuf.at[s, wrow(d)], (depth[o], s, m))
-
+    limit = jnp.minimum(s, span_ref[0])
+
+    def score(span):
+        for h in range(heads):
+            lanes = slice(h * HEAD, (h + 1) * HEAD)
+            raw = lax.dot_general(
+                kbuf[span, :, lanes], q_ref[:, lanes], (((1,), (1,)), ((), ())),
+                preferred_element_type=jnp.float32) * (HEAD ** -0.5)
+            sbuf[h, span] = jnp.where(jnp.full(raw.shape, span, jnp.int32) <= limit, raw, -jnp.inf)
+
+    def turn(span):
+        for h in range(heads):
+            lanes = slice(h * HEAD, (h + 1) * HEAD)
+            tbuf[h, span] = vbuf[span, :, lanes].T
+
+    early[1].wait()
+    local[0].wait()
+    score(s)
+    local[1].wait()
+    turn(s)
     arrive("ka", kbuf.at[first])
     send("kc", kbuf.at[first], kbuf.at[first], dev["b"])
+    score(first)
     arrive("va", vbuf.at[first])
     send("vc", vbuf.at[first], vbuf.at[first], dev["b"])
     for p in ("a", "b"):
         send("t" + p, cot_ref.at[mine], cbuf.at[s, mine], dev[p])
-    local[0].wait()
-    local[1].wait()
+    turn(first)
     arrive("kb", kbuf.at[second])
+    score(second)
     arrive("vb", vbuf.at[second])
+    turn(second)
     arrive("kc", kbuf.at[far])
+    score(far)
+
+    probs = []
+    for h in range(heads):
+        scores = sbuf[h].reshape(PLANE * tok, tok)
+        weights = jnp.exp(scores - jnp.max(scores, axis=0, keepdims=True))
+        scale = 1.0 / jnp.sum(weights, axis=0, keepdims=True)
+        probs.append((weights * scale).astype(jnp.bfloat16))
     arrive("vc", vbuf.at[far])
-
-    limit = jnp.minimum(s, span_ref[0])
-    visible = lax.broadcasted_iota(jnp.int32, (PLANE, tok, tok), 0) <= limit
+    turn(far)
     columns = []
     for h in range(heads):
-        lanes = slice(h * HEAD, (h + 1) * HEAD)
-        keys = kbuf[:, :, lanes].reshape(PLANE * tok, HEAD)
-        values = vbuf[:, :, lanes].reshape(PLANE * tok, HEAD)
-        scores = lax.dot_general(
-            keys, q_ref[:, lanes], (((1,), (1,)), ((), ())),
-            preferred_element_type=jnp.float32) * (HEAD ** -0.5)
-        scores = jnp.where(visible, scores.reshape(PLANE, tok, tok), -jnp.inf)
-        scores = scores.reshape(PLANE * tok, tok)
-        weights = jnp.exp(scores - jnp.max(scores, axis=0, keepdims=True))
-        total = jnp.sum(weights, axis=0, keepdims=True)
-        probs = (weights / total).astype(jnp.bfloat16)
-        columns.append(lax.dot_general(
-            values, probs, (((0,), (0,)), ((), ())), preferred_element_type=jnp.float32))
+        values = jnp.concatenate([tbuf[h, j] for j in range(PLANE)], axis=1)
+        columns.append(jnp.dot(values, probs[h], preferred_element_type=jnp.float32))
     turned = jnp.concatenate(columns, axis=0)
-    attn[...] = turned.astype(jnp.bfloat16)
     grouped = turned.reshape(dp_count, PLANE, piece, tok)
     for t in range(PLANE):
         asend[t] = grouped[:, t].reshape(dp_count * piece, tok).astype(jnp.bfloat16)
     for p, i in (("c", far), ("a", first), ("b", second)):
         send("o" + p, asend.at[i], abuf.at[s], dev[p])
     abuf[s] = asend[s]
+    attn[...] = turned.T.astype(jnp.bfloat16)
 
     arrive("ta", cbuf.at[first, mine])
     send("tc", cbuf.at[first, mine], cbuf.at[first, mine], dev["b"])
@@ -143,7 +166,7 @@
 
     def project(slot, column):
         mix[slot] = lax.dot_general(
-            attn[...], wbuf[column], (((0,), (0,)), ((), ())),
+            attn[...], wbuf[column], (((1,), (0,)), ((), ())),
             preferred_element_type=jnp.float32)
         msend[slot] = mix[slot, other].astype(jnp.bfloat16)
         send(f"m{slot}", msend.at[slot], mrecv.at[slot], sibling)
@@ -219,14 +242,18 @@
             jax.ShapeDtypeStruct((tok // 2, model), bf16),
             jax.ShapeDtypeStruct((piece, model), f32),
         ),
-        in_specs=[vmem, anywhere, anywhere, anywhere, vmem, smem, smem, anywhere],
+        in_specs=[anywhere] * 5 + [smem, smem, anywhere],
         out_specs=(vmem, vmem),
         scratch_shapes=[
+            pltpu.VMEM((tok, width), bf16),
+            pltpu.VMEM(gate_table.shape, f32),
             pltpu.VMEM((PLANE, tok, width), bf16),
             pltpu.VMEM((PLANE, tok, width), bf16),
             pltpu.VMEM((PLANE, dp_count * wrows, model // PLANE), bf16),
             pltpu.VMEM((PLANE, tok, model), bf16),
-            pltpu.VMEM((width, tok), bf16),
+            pltpu.VMEM((tok, width), bf16),
+            pltpu.VMEM((width // HEAD, PLANE, tok, tok), f32),
+            pltpu.VMEM((width // HEAD, PLANE, HEAD, tok), bf16),
             pltpu.VMEM((PLANE, dp_count * piece, tok), bf16),
             pltpu.VMEM((PLANE, dp_count * piece, tok), bf16),
             pltpu.VMEM((dp_count, piece, model), f32),
@@ -236,12 +263,12 @@
             pltpu.VMEM((PLANE, tok // 2, model // PLANE), bf16),
             pltpu.VMEM((PLANE, tok // 2, model // PLANE), bf16),
             pltpu.VMEM((1, model), f32),
-            pltpu.SemaphoreType.DMA((3 + PLANE,)),
+            pltpu.SemaphoreType.DMA((5 + PLANE,)),
             pltpu.SemaphoreType.DMA((copies,)),
             pltpu.SemaphoreType.DMA((copies,)),
         ],
         compiler_params=pltpu.CompilerParams(
-            collective_id=0, has_side_effects=True, vmem_limit_bytes=48 * 2**20),
+            collective_id=0, has_side_effects=True, vmem_limit_bytes=62 * 2**20),
     )(queries[0], keys[0], values[0], proj_weight[0], gate_table, timestep, span_index, cotangent[0])
     return output[None], grad.reshape(1, -1, 128)
 

time: 41.8 us -> 38.4 us (0.919)
  local copies, waits for them, and re-layouts: 6.71 us -> 2.3 us
  Pallas kernels: 32.8 us -> 34 us
    unnamed x13 -> x3, local copies, waits for them, and re-layouts: 6.04 us -> 0.68 us
    pallas_call x1, Pallas kernels: 32.8 us -> 34 us  [fused_local(): pl.pallas_call(functools.partial(fused, dp_count), out_shape=(jax.ShapeDt...]
    reshape x1, local copies, waits for them, and re-layouts: 0.67 us -> 1.62 us  [fused_local(): return (output[None], grad.reshape(1, -1, 128))]
where the time goes in v2:
time: 38.4 us; the launch traced here: 38.2 us
  Pallas kernels  34 us (89%)
  local copies, waits for them, and re-layouts  2.3 us (6%)
  between operations  1.94 us (5%)
    pallas_call x1, Pallas kernels, fused_local(): pl.pallas_call(functools.partial(fused, dp_count), out_shape=(jax.ShapeDt...  34 us
    reshape x1, local copies, waits for them, and re-layouts, fused_local(): return (output[None], grad.reshape(1, -1, 128))  1.62 us

profile of v2, /device:TPU:1, one launch (start us, length us, event | category | flops | bytes accessed | tf_op | source)
XLA Modules:
  0.0 38.2 jit_solution(2484941498297991250)
XLA Ops:
  1.9 34.0 %shard_map.95 = (bf16[64,1536]{1,0:T(8,128)(2,1)}, f32[24,1536]{1,0:T(8,128)}) custom-call(bf16[128,384]{1,0:T(8,128)(2,1)} %bitcast.9, bf16[128,384]{1,0:T(8,128)(2,1)} %bitcast.10, bf16[128,384]{1,0:T(8,128)(2,1)} %bitcast.11, bf16[96,1536]{1,0:T(8,128)(2,1)} %bitcast.7, f32[4,1536]{1,0:T(4,128)} %gate_hbm.1, s32[1]{0:T(128)S(6)} %copy.11.time_ref, ...), custom_call_target="tpu_custom_call" | custom-call | tf_op jit(solution)/shard_map/pallas_call | solution.py:239
  35.9 0.0 copy-start
  35.9 1.6 %reshape.7 = f32[1,288,128]{2,1,0:T(8,128)} reshape(f32[24,1536]{1,0:T(8,128)} %get-tuple-element.5) | data formatting | bytes 294912 | tf_op jit(solution)/shard_map/reshape | solution.py:273
  37.5 0.0 copy-done
  37.5 0.7 %copy.13 = bf16[1,64,1536]{2,1,0:T(8,128)(2,1)} copy(bf16[1,64,1536]{2,1,0:T(8,128)(2,1)S(1)} %bitcast.8) | data formatting | bytes 393216
Async XLA Ops:
  35.9 1.6 %copy-start = (bf16[64,1536]{1,0:T(8,128)(2,1)S(1)}, bf16[64,1536]{1,0:T(8,128)(2,1)}, u32[]{:S(2)}) copy-start(bf16[64,1536]{1,0:T(8,128)(2,1)} %get-tuple-element.4) | copy-start | bytes 589828

commit v3 on v2

--- a/solution.py
+++ b/solution.py
@@ -171,12 +171,11 @@
         msend[slot] = mix[slot, other].astype(jnp.bfloat16)
         send(f"m{slot}", msend.at[slot], mrecv.at[slot], sibling)
 
+    arrive("tc", cbuf.at[far, mine])
+    send("sc", cbuf.at[far, mine], cbuf.at[far, mine], sibling)
     for copy in local[2:]:
         copy.wait()
     project(0, s)
-
-    arrive("tc", cbuf.at[far, mine])
-    send("sc", cbuf.at[far, mine], cbuf.at[far, mine], sibling)
     for p, i in (("c", far), ("a", first), ("b", second)):
         arrive("o" + p, abuf.at[i])
     for p, i in (("a", second), ("b", first), ("c", far)):

time: 38.4 us -> 38.6 us (level)
  no operation moved by 1% of the time
where the time goes in v3:
time: 38.6 us; the launch traced here: 38.5 us
  Pallas kernels  34.2 us (89%)
  local copies, waits for them, and re-layouts  2.3 us (6%)
  between operations  1.94 us (5%)
    pallas_call x1, Pallas kernels, fused_local(): pl.pallas_call(functools.partial(fused, dp_count), out_shape=(jax.ShapeDt...  34.2 us
    reshape x1, local copies, waits for them, and re-layouts, fused_local(): return (output[None], grad.reshape(1, -1, 128))  1.62 us

profile of v3, /device:TPU:1, one launch (start us, length us, event | category | flops | bytes accessed | tf_op | source)
XLA Modules:
  0.0 38.5 jit_solution(4837449916799458140)
XLA Ops:
  1.9 34.2 %shard_map.95 = (bf16[64,1536]{1,0:T(8,128)(2,1)}, f32[24,1536]{1,0:T(8,128)}) custom-call(bf16[128,384]{1,0:T(8,128)(2,1)} %bitcast.9, bf16[128,384]{1,0:T(8,128)(2,1)} %bitcast.10, bf16[128,384]{1,0:T(8,128)(2,1)} %bitcast.11, bf16[96,1536]{1,0:T(8,128)(2,1)} %bitcast.7, f32[4,1536]{1,0:T(4,128)} %gate_hbm.1, s32[1]{0:T(128)S(6)} %copy.11.time_ref, ...), custom_call_target="tpu_custom_call" | custom-call | tf_op jit(solution)/shard_map/pallas_call | solution.py:238
  36.2 0.0 copy-start
  36.2 1.6 %reshape.7 = f32[1,288,128]{2,1,0:T(8,128)} reshape(f32[24,1536]{1,0:T(8,128)} %get-tuple-element.5) | data formatting | bytes 294912 | tf_op jit(solution)/shard_map/reshape | solution.py:272
  37.8 0.0 copy-done
  37.8 0.7 %copy.13 = bf16[1,64,1536]{2,1,0:T(8,128)(2,1)} copy(bf16[1,64,1536]{2,1,0:T(8,128)(2,1)S(1)} %bitcast.8) | data formatting | bytes 393216
Async XLA Ops:
  36.2 1.6 %copy-start = (bf16[64,1536]{1,0:T(8,128)(2,1)S(1)}, bf16[64,1536]{1,0:T(8,128)(2,1)}, u32[]{:S(2)}) copy-start(bf16[64,1536]{1,0:T(8,128)(2,1)} %get-tuple-element.4) | copy-start | bytes 589828

commit v4 on v3

--- a/solution.py
+++ b/solution.py
@@ -34,6 +34,9 @@
     first, second, far = at(1 - m, m), at(m, 1 - m), at(1, 1)
     dev = {p: (d, i, m) for p, i in (("a", first), ("b", second), ("c", far))}
     sibling = (d, s, 1 - m)
+    own = 2 * lax.rem(x + y, 2)
+    rest = 2 - own
+    beside = ((d, at(1, 0), m), (d, at(0, 1), m))
     depth = [lax.rem(d + o, dp_count) for o in range(dp_count)]
     depth_from = [lax.rem(d + dp_count - o, dp_count) for o in range(dp_count)]
 
@@ -91,7 +94,9 @@
     for p in ("a", "b"):
         send("v" + p, v_ref, vbuf.at[s], dev[p])
     for o in range(1, dp_count):
-        send(f"wz{o}", w_ref.at[:, wcol(s)], wbuf.at[s, wrow(d)], (depth[o], s, m))
+        for j in range(2):
+            send(f"wz{j}{o}", w_ref.at[:, wcol(own + j)], wbuf.at[own + j, wrow(d)],
+                 (depth[o], s, m))
 
     early[0].wait()
     table = gate_ref[...]
@@ -156,11 +161,6 @@
     arrive("ta", cbuf.at[first, mine])
     send("tc", cbuf.at[first, mine], cbuf.at[first, mine], dev["b"])
     send("sa", cbuf.at[first, mine], cbuf.at[first, mine], sibling)
-    for o in range(1, dp_count):
-        block = wbuf.at[s, wrow(depth_from[o])]
-        arrive(f"wz{o}", block)
-        for p in ("a", "b"):
-            send(f"w{p}{o}", block, block, dev[p])
     arrive("tb", cbuf.at[second, mine])
     send("sb", cbuf.at[second, mine], cbuf.at[second, mine], sibling)
 
@@ -173,9 +173,14 @@
 
     arrive("tc", cbuf.at[far, mine])
     send("sc", cbuf.at[far, mine], cbuf.at[far, mine], sibling)
+    for j in range(2):
+        for o in range(1, dp_count):
+            block = wbuf.at[own + j, wrow(depth_from[o])]
+            arrive(f"wz{j}{o}", block)
+            send(f"wn{j}{o}", block, block, beside[j])
     for copy in local[2:]:
         copy.wait()
-    project(0, s)
+    project(0, own)
     for p, i in (("c", far), ("a", first), ("b", second)):
         arrive("o" + p, abuf.at[i])
     for p, i in (("a", second), ("b", first), ("c", far)):
@@ -195,17 +200,11 @@
         for o in range(1, dp_count):
             send(f"r{c}{o}", rsend.at[c, depth[o]], rbuf.at[c, o - 1], (depth[o], s, m))
 
-    for o in range(1, dp_count):
-        block = wbuf.at[first, wrow(depth_from[o])]
-        arrive(f"wa{o}", block)
-        send(f"wc{o}", block, block, dev["b"])
-    for o in range(1, dp_count):
-        arrive(f"wb{o}", wbuf.at[second, wrow(depth_from[o])])
-    project(1, at(1, 0))
-    project(2, at(0, 1))
-    for o in range(1, dp_count):
-        arrive(f"wc{o}", wbuf.at[far, wrow(depth_from[o])])
-    project(3, far)
+    project(1, own + 1)
+    for j in range(2):
+        for o in range(1, dp_count):
+            arrive(f"wn{j}{o}", wbuf.at[rest + j, wrow(depth_from[o])])
+        project(2 + j, rest + j)
 
     for c in range(CHUNKS):
         lanes = slice(c * part, (c + 1) * part)
@@ -216,7 +215,7 @@
             total += jnp.concatenate([got[:piece], got[piece:]], axis=1)
         grad_ref[:, lanes] = total
 
-    for slot, column in enumerate((s, at(1, 0), at(0, 1), far)):
+    for slot, column in enumerate((own, own + 1, rest, rest + 1)):
         arrive(f"m{slot}", mrecv.at[slot])
         whole = mix[slot, mine] + mrecv[slot].astype(jnp.float32)
         out_ref[:, wcol(column)] = (grow[:, wcol(column)] * whole).astype(jnp.bfloat16)

time: 38.6 us -> 37.8 us (0.979)
  Pallas kernels: 34.2 us -> 33.4 us
    pallas_call x1, Pallas kernels: 34.2 us -> 33.4 us  [fused_local(): pl.pallas_call(functools.partial(fused, dp_count), out_shape=(jax.ShapeDt...]
where the time goes in v4:
time: 37.8 us; the launch traced here: 37.7 us
  Pallas kernels  33.4 us (88%)
  local copies, waits for them, and re-layouts  2.3 us (6%)
  between operations  1.94 us (5%)
    pallas_call x1, Pallas kernels, fused_local(): pl.pallas_call(functools.partial(fused, dp_count), out_shape=(jax.ShapeDt...  33.4 us
    reshape x1, local copies, waits for them, and re-layouts, fused_local(): return (output[None], grad.reshape(1, -1, 128))  1.62 us

profile of v4, /device:TPU:1, one launch (start us, length us, event | category | flops | bytes accessed | tf_op | source)
XLA Modules:
  0.0 37.7 jit_solution(1254339385109083077)
XLA Ops:
  1.9 33.4 %shard_map.95 = (bf16[64,1536]{1,0:T(8,128)(2,1)}, f32[24,1536]{1,0:T(8,128)}) custom-call(bf16[128,384]{1,0:T(8,128)(2,1)} %bitcast.9, bf16[128,384]{1,0:T(8,128)(2,1)} %bitcast.10, bf16[128,384]{1,0:T(8,128)(2,1)} %bitcast.11, bf16[96,1536]{1,0:T(8,128)(2,1)} %bitcast.7, f32[4,1536]{1,0:T(4,128)} %gate_hbm.1, s32[1]{0:T(128)S(6)} %copy.11.time_ref, ...), custom_call_target="tpu_custom_call" | custom-call | tf_op jit(solution)/shard_map/pallas_call | solution.py:237
  35.4 0.0 copy-start
  35.4 1.6 %reshape.7 = f32[1,288,128]{2,1,0:T(8,128)} reshape(f32[24,1536]{1,0:T(8,128)} %get-tuple-element.5) | data formatting | bytes 294912 | tf_op jit(solution)/shard_map/reshape | solution.py:271
  37.0 0.0 copy-done
  37.0 0.7 %copy.13 = bf16[1,64,1536]{2,1,0:T(8,128)(2,1)} copy(bf16[1,64,1536]{2,1,0:T(8,128)(2,1)S(1)} %bitcast.8) | data formatting | bytes 393216
Async XLA Ops:
  35.4 1.6 %copy-start = (bf16[64,1536]{1,0:T(8,128)(2,1)S(1)}, bf16[64,1536]{1,0:T(8,128)(2,1)}, u32[]{:S(2)}) copy-start(bf16[64,1536]{1,0:T(8,128)(2,1)} %get-tuple-element.4) | copy-start | bytes 589828
